TPU v7x, 256 devices: a whole 4x4x8 slice. The times are simulated.
256 devices in a mesh: theta: 8 (over z_hi, core), phi: 4 (over y), box: 8 (over z_lo, x).
Axes of the slice: x: 4, y: 4, z: 8 (z_hi: 4, z_lo: 2; z = z_hi * 2 + z_lo), core: 2. Of those that a mesh axis runs over, the one named last changes fastest.
Arguments:
- pattern: float32 [2, 64, 1024, 2048], P(None, 'box', 'theta', 'phi'), may hold values from -6 to 6
- legendre: bfloat16 [4, 128, 512, 512], P('phi', 'theta'), may hold values from -0.005859375 to 0.005859375
- degree: int32 [64], P('box'), may hold values from 256 to 512, as said below
- owner: int32 [64], replicated, may hold values from 0 to 63, as said below
Outputs:
- harmonics: bfloat16 [4, 64, 512, 512], P(None, 'box', 'theta', 'phi')
Inputs may be any that keep to these rules, and one draw needn't show every extreme that they name: Some box has degree 512. owner is a permutation of the box numbers; of the 8 boxes b with the same b // 8, exactly 1 have owner[b] // 8 equal to each value 0 to 7.
All inputs are finite; a program needn't handle non-finite values.
Results may differ from a plain program's by a relative error of at most 0.0049.
Values may be sent and summed in bfloat16 or wider, within the bound.
A program may use at most 128 MiB of HBM per device.

v0:
```python
import math

import jax
import jax.numpy as jnp
from jax import lax
from jax.sharding import PartitionSpec as P


def local(pattern, legendre, degree, owner):
    theta_count = lax.axis_size("theta")
    phi_count = lax.axis_size("phi")
    box_groups = lax.axis_size("box")
    theta_index = lax.axis_index("theta")
    phi_index = lax.axis_index("phi")
    box_index = lax.axis_index("box")
    box_count = pattern.shape[1]
    row_count = pattern.shape[2]
    col_count = pattern.shape[3]
    per_device = legendre.shape[1]
    half_rows = legendre.shape[2]
    degree_count = legendre.shape[3]
    group_orders = per_device * theta_count
    all_orders = group_orders * phi_count
    total_cols = col_count * phi_count
    own_columns = phi_index * col_count + jnp.arange(col_count, dtype=jnp.int32)
    slot_ids = jnp.arange(all_orders, dtype=jnp.int32)
    slot_target = slot_ids // per_device
    owner_orders = (
        slot_target % phi_count * group_orders
        + slot_target // phi_count * per_device
        + slot_ids % per_device
    )
    phase_ids = owner_orders[:, None] * own_columns[None, :] % total_cols
    angles = phase_ids.astype(jnp.float32) * (2.0 * math.pi / total_cols)
    trig_table = jnp.stack([jnp.cos(angles), jnp.sin(angles)])
    terms = jnp.einsum(
        "skp,abtp->ksabt",
        trig_table,
        pattern,
        precision=lax.Precision.HIGHEST,
        preferred_element_type=jnp.float32,
    )
    partial_terms = terms.reshape(all_orders, 4, box_count, pattern.shape[2])
    received = lax.all_to_all(
        partial_terms, ("theta", "phi"), split_axis=0, concat_axis=3, tiled=True
    )
    received = received.reshape(per_device, 4, box_count, theta_count, phi_count, row_count)
    spectrum = jnp.sum(received, axis=4).reshape(per_device, 4, box_count, theta_count * row_count)
    full_rows = spectrum.shape[3]
    north_rows = spectrum[..., : full_rows // 2]
    south_rows = jnp.flip(spectrum[..., full_rows // 2 :], axis=3)
    even_part = (north_rows + south_rows).astype(jnp.bfloat16)
    odd_part = (north_rows - south_rows).astype(jnp.bfloat16)
    order_ids = (
        phi_index * group_orders
        + theta_index * per_device
        + jnp.arange(per_device, dtype=jnp.int32)
    )
    parity = (order_ids % 2).reshape(per_device, 1, 1, 1)
    first_src = jnp.where(parity == 0, even_part, odd_part)
    second = jnp.where(parity == 0, odd_part, even_part)
    tables = legendre.reshape(per_device, half_rows, degree_count // 2, 2)
    low_half = jnp.einsum(
        "kcbt,ktj->cbjk", first_src, tables[..., 0], preferred_element_type=jnp.float32
    )
    high_half = jnp.einsum(
        "kcbt,ktj->cbjk", second, tables[..., 1], preferred_element_type=jnp.float32
    )
    result = jnp.stack([low_half, high_half], axis=3).reshape(
        4, box_count, degree_count, per_device
    )
    keep_mask = jnp.arange(degree_count, dtype=jnp.int32)[None, :, None] < degree[:, None, None]
    kept = jnp.where(keep_mask[None], result, 0.0).astype(jnp.bfloat16)
    each_pair = box_count // box_groups
    positions = owner.reshape(box_groups, box_count)
    target_all = positions // box_count
    order_all = jnp.argsort(target_all, axis=1, stable=True)
    outgoing = jnp.take(kept, order_all[box_index], axis=1)
    my_boxes = lax.dynamic_slice_in_dim(order_all, box_index * each_pair, each_pair, 1)
    slot_list = (jnp.take_along_axis(positions, my_boxes, axis=1) % box_count).reshape(-1)
    inverse = jnp.argsort(slot_list)
    rows_back = lax.all_to_all(outgoing, "theta", split_axis=2, concat_axis=3, tiled=True)
    arrived = lax.all_to_all(rows_back, "box", split_axis=1, concat_axis=1, tiled=True)
    return jnp.take(arrived, inverse, axis=1)


def solution(mesh):
    in_specs = (P(None, "box", "theta", "phi"), P("phi", "theta", None, None), P("box"), P())
    out_specs = P(None, "box", "theta", "phi")
    return jax.shard_map(local, mesh=mesh, in_specs=in_specs, out_specs=out_specs, check_vma=False)
```

profile of v0, /device:TPU:1, one launch (start us, length us, event | category | flops | bytes accessed | tf_op | source)
XLA Modules:
  0.0 312.0 jit_solution(5039812416324622302)
XLA Ops:
  0.0 4.1 %fusion.20 = (f32[1,512,512]{2,1,0:T(8,128)S(1)}, f32[1,512,512]{2,1,0:T(8,128)S(1)}) fusion(s32[512]{0:T(512)S(1)} %get-tuple-element.16, s32[512]{0:T(512)S(1)} %get-tuple-element.15), kind=kLoop, calls=%fused_computation.32 | loop fusion | flops 3670016 | bytes 2101248 | tf_op jit(solution)/shard_map/cos | solution.py:35
  4.2 16.4 %fusion.4 = f32[2,512,2,8,128]{4,1,3,2,0:T(8,128)S(1)} fusion(f32[2,8,128,512]{3,2,1,0:T(8,128)} %param.4, f32[1,512,512]{2,1,0:T(8,128)S(1)} %get-tuple-element.14, f32[1,512,512]{2,1,0:T(8,128)S(1)} %get-tuple-element.13), kind=kOutput, calls=%fused_computation.7 | convolution fusion | flops 12885426176 | bytes 14680064 | tf_op jit(solution)/shard_map/skp,abtp->ksabt/dot_general | solution.py:36
  20.6 8.1 %copy.48 = f32[512,4,8,128]{3,2,1,0:T(8,128)} copy(f32[512,4,8,128]{3,0,2,1:T(8,128)S(1)} %bitcast.72) | data formatting | bytes 16777216 | tf_op jit(solution)/shard_map/reshape | solution.py:43
  28.7 12.8 %all-to-all-start = ((f32[512,4,8,128]{3,2,1,0:T(8,128)}), f32[512,4,8,128]{3,2,1,0:T(8,128)}, u32[]{:S(2)}, u32[]{:S(2)}) async-start(f32[512,4,8,128]{3,2,1,0:T(8,128)} %copy.48), calls=%async_computation | async-start | bytes 16777216 | tf_op jit(solution)/shard_map/all_to_all | solution.py:44
  41.5 14.9 %copy.51 = bf16[1,16,512,512]{2,1,3,0:T(8,128)(2,1)} copy(bf16[1,16,512,512]{3,2,1,0:T(8,128)(2,1)} %param.5) | data formatting | bytes 16777216 | tf_op args[1]
  56.4 5.9 %fusion.48 = (bf16[16,512,256,1]{1,0,3,2:T(8,128)(2,1)}, bf16[16,512,256,1]{1,0,3,2:T(8,128)(2,1)}) fusion(bf16[16,512,256,2]{1,0,3,2:T(8,128)(2,1)} %bitcast.73), kind=kLoop, calls=%fused_computation.94 | loop fusion | bytes 16777216 | tf_op jit(solution)/shard_map/slice | solution.py:64
  62.4 7.5 %copy.66 = bf16[16,512,256,1]{2,1,0,3:T(8,128)(2,1)} copy(bf16[16,512,256,1]{1,0,3,2:T(8,128)(2,1)} %get-tuple-element.9) | data formatting | bytes 8388608
  69.9 7.5 %copy.67 = bf16[16,512,256,1]{2,1,0,3:T(8,128)(2,1)} copy(bf16[16,512,256,1]{1,0,3,2:T(8,128)(2,1)} %get-tuple-element.10) | data formatting | bytes 8388608
  79.3 145.7 %all-to-all-done = f32[512,4,8,128]{3,2,1,0:T(8,128)} async-done(((f32[512,4,8,128]{3,2,1,0:T(8,128)}), f32[512,4,8,128]{3,2,1,0:T(8,128)}, u32[]{:S(2)}, u32[]{:S(2)}) %all-to-all-start) | async-done | bytes 8388640 | tf_op jit(solution)/shard_map/all_to_all | solution.py:44
  225.0 6.0 %reduce = f32[16,4,8,8,128]{4,2,1,0,3:T(8,128)} reduce(f32[16,4,8,8,4,128]{5,2,1,0,4,3:T(8,128)} %bitcast.13, f32[]{:T(128)} %constant.160.clone.1), dimensions={4}, to_apply=%region_2.3 | reduce | flops 1572864 | bytes 10485764 | tf_op jit(solution)/shard_map/reduce_sum | solution.py:48
  231.0 1.9 copy_bitcast_fusion
  232.9 1.1 slice.23
  234.0 2.3 rev.4
  236.7 3.1 %fusion.8 = bf16[4,8,256,1,16]{2,1,0,4,3:T(8,128)(2,1)S(1)} fusion(bf16[16,512,256,1]{2,1,0,3:T(8,128)(2,1)} %copy.66, bf16[16,4,8,512]{3,2,1,0:T(8,128)(2,1)S(1)} %get-tuple-element.11, bf16[16,4,8,512]{3,2,1,0:T(8,128)(2,1)S(1)} %get-tuple-element.12, pred[16]{0:T(512)(128)(4,1)S(1)} %fusion.42), kind=kOutput, calls=%fused_computation.18 | convolution fusion | flops 134479872 | bytes 5505040 | tf_op jit(solution)/shard_map/kcbt,ktj->cbjk/dot_general | solution.py:63
  240.7 4.9 %copy.54 = bf16[4,8,256,2,16]{4,1,3,2,0:T(8,128)(2,1)} copy(bf16[4,8,256,2,16]{2,1,0,4,3:T(8,128)(2,1)S(1)} %pad_maximum_fusion) | data formatting | bytes 1048576 | tf_op jit(solution)/shard_map/stack | solution.py:69
  245.6 4.4 %copy.55 = bf16[4,8,512,16]{2,3,1,0:T(8,128)(2,1)S(1)} copy(bf16[4,8,512,16]{3,1,2,0:T(8,128)(2,1)} %bitcast.75) | data formatting | bytes 1048576 | tf_op jit(solution)/shard_map/reshape | solution.py:69
  250.8 5.4 %copy.56 = bf16[4,8,512,16]{3,0,1,2:T(4,128)(2,1)} copy(bf16[4,8,512,16]{2,3,0,1:T(8,128)(2,1)S(1)} %select_bitcast_fusion.1) | data formatting | bytes 1048576 | tf_op jit(solution)/shard_map/jit(_take)/select_n | solution.py:78
  256.2 5.7 %reshape.352 = bf16[8,2,16384]{2,1,0:T(2,128)(2,1)S(1)} reshape(bf16[512,8,4,16]{3,2,1,0:T(4,128)(2,1)} %bitcast.76) | data formatting | bytes 1048576
  261.9 20.7 %all_to_all.38 = bf16[8,2,16384]{2,1,0:T(2,128)(2,1)S(1)} all-to-all(bf16[8,2,16384]{2,1,0:T(2,128)(2,1)S(1)} %reshape.352), channel_id=1, replica_groups=mesh['theta'=8,'phi'=4,'box'=8] {'theta'}, dimensions={0} | all-to-all | bytes 1048576 | tf_op jit(solution)/shard_map/all_to_all | solution.py:82
  282.7 4.1 %reshape.353 = bf16[512,8,4,16]{3,2,1,0:T(4,128)(2,1)} reshape(bf16[8,2,16384]{2,1,0:T(2,128)(2,1)S(1)} %all_to_all.38) | data formatting | bytes 1048576
  286.8 5.6 %copy.57 = bf16[4,8,8,64,16]{3,4,2,1,0:T(8,128)(2,1)S(1)} copy(bf16[4,8,8,64,16]{4,0,1,3,2:T(4,128)(2,1)} %bitcast.74) | data formatting | bytes 1048576 | tf_op jit(solution)/shard_map/all_to_all | solution.py:82
  292.4 1.1 copy.58
  293.6 9.0 %all-to-all-start.2 = ((bf16[4,8,64,128]{3,2,0,1:T(8,128)(2,1)}), bf16[4,8,64,128]{3,2,0,1:T(8,128)(2,1)S(1)}, u32[]{:S(2)}, u32[]{:S(2)}) async-start(bf16[4,8,64,128]{3,2,0,1:T(8,128)(2,1)} %copy.58), calls=%async_computation.2 | async-start | bytes 1048576 | tf_op jit(solution)/shard_map/all_to_all | solution.py:83
  303.6 6.8 %all-to-all-done.2 = bf16[4,8,64,128]{3,2,0,1:T(8,128)(2,1)S(1)} async-done(((bf16[4,8,64,128]{3,2,0,1:T(8,128)(2,1)}), bf16[4,8,64,128]{3,2,0,1:T(8,128)(2,1)S(1)}, u32[]{:S(2)}, u32[]{:S(2)}) %all-to-all-start.2) | async-done | bytes 524320 | tf_op jit(solution)/shard_map/all_to_all | solution.py:83
  (38 shorter events, 6.5 us)
Async XLA Ops:
  28.7 196.3 %all-to-all-start = ((f32[512,4,8,128]{3,2,1,0:T(8,128)}), f32[512,4,8,128]{3,2,1,0:T(8,128)}, u32[]{:S(2)}, u32[]{:S(2)}) async-start(f32[512,4,8,128]{3,2,1,0:T(8,128)} %copy.48), calls=%async_computation | async-start | bytes 16777216 | tf_op jit(solution)/shard_map/all_to_all | solution.py:44
  69.9 7.5 %copy-start.1 = (s32[64]{0:T(128)S(1)}, s32[64]{0:T(128)}, u32[]{:S(2)}) copy-start(s32[64]{0:T(128)} %param.7) | copy-start | bytes 772
  69.9 9.3 %copy-start.2 = (s32[8]{0:T(128)S(1)}, s32[8]{0:T(128)}, u32[]{:S(2)}) copy-start(s32[8]{0:T(128)} %param.6) | copy-start | bytes 100
  236.3 3.5 %copy-start = (bf16[16,512,256,1]{2,1,0,3:T(8,128)(2,1)S(1)}, bf16[16,512,256,1]{2,1,0,3:T(8,128)(2,1)}, u32[]{:S(2)}) copy-start(bf16[16,512,256,1]{2,1,0,3:T(8,128)(2,1)} %copy.67) | copy-start | bytes 12582916
  293.6 16.8 %all-to-all-start.2 = ((bf16[4,8,64,128]{3,2,0,1:T(8,128)(2,1)}), bf16[4,8,64,128]{3,2,0,1:T(8,128)(2,1)S(1)}, u32[]{:S(2)}, u32[]{:S(2)}) async-start(bf16[4,8,64,128]{3,2,0,1:T(8,128)(2,1)} %copy.58), calls=%async_computation.2 | async-start | bytes 1048576 | tf_op jit(solution)/shard_map/all_to_all | solution.py:83
where the time goes:
time: 314 us; the launch traced here: 312 us
  waiting for transfers between devices  152 us (48%)
  local copies, waits for them, and re-layouts  83.7 us (27%)
  starting transfers between devices  21.8 us (7%)
  blocking collectives  20.7 us (7%)
  matrix products  20.4 us (6%)
  other arithmetic  12.8 us (4%)
    all_to_all x1, waiting for transfers between devices, local(): lax.all_to_all(partial_terms, ('theta', 'phi'), split_axis=0, concat_axis...  146 us
    unnamed x12, local copies, waits for them, and re-layouts  39.9 us
    all_to_all x1, blocking collectives, local(): lax.all_to_all(outgoing, 'theta', split_axis=2, concat_axis=3, tiled=True)  20.7 us
    dot_general x1, matrix products, local(): jnp.einsum('skp,abtp->ksabt', trig_table, pattern, precision=lax.Precisio...  16.4 us
    all_to_all x1, starting transfers between devices, local(): lax.all_to_all(partial_terms, ('theta', 'phi'), split_axis=0, concat_axis...  12.8 us
    all_to_all x1, starting transfers between devices, local(): lax.all_to_all(rows_back, 'box', split_axis=1, concat_axis=1, tiled=True)  8.99 us
    reshape x1, local copies, waits for them, and re-layouts, local(): partial_terms = terms.reshape(all_orders, 4, box_count, pattern.shape[2])  8.07 us
    all_to_all x2, local copies, waits for them, and re-layouts, local(): lax.all_to_all(outgoing, 'theta', split_axis=2, concat_axis=3, tiled=True)  6.77 us
  transfers between devices with their start and end apart: 2, of which 2 were waited for; matrix products, arithmetic and copies ran while one was open for 12% of the time, Pallas kernels for 0%

commit v1 on v0

v1 whole, which is shorter than its diff:
```python
import functools
import math

import jax
import jax.numpy as jnp
import numpy as np
from jax import lax
from jax.experimental import pallas as pl
from jax.experimental.pallas import tpu as pltpu
from jax.sharding import PartitionSpec as P

MESH = pl.DeviceIdType.MESH
NTHETA, NPHI, NBOX = 8, 4, 8
CHUNKS = 4
PLANE = NTHETA * NPHI
ROWS = 128
COLS = 512
ORDERS = 16
BF = jnp.bfloat16
F32 = jnp.float32


def trig_table():
    total = NPHI * COLS
    orders = np.arange(PLANE * ORDERS).reshape(PLANE, 1, ORDERS, 1)
    angle = 2.0 * math.pi * (orders * np.arange(total) % total) / total
    table = np.concatenate([np.cos(angle), np.sin(angle)], axis=1)
    table = table.reshape(PLANE * 2 * ORDERS, NPHI, COLS).transpose(1, 0, 2)
    return np.ascontiguousarray(table).astype(jnp.bfloat16)


def dot(a, b):
    return jnp.dot(a, b, preferred_element_type=F32)


def dot_nt(a, b):
    return lax.dot_general(a, b, (((1,), (1,)), ((), ())), preferred_element_type=F32)


def iota(shape, dim):
    return lax.broadcasted_iota(jnp.int32, shape, dim)


def kernel(
    pattern, trig, table, degree, owner, out,
    pat, xsend, xrecv, trig_v, table_v, zsend, zrecv, lhs, prod, fsend, frecv,
    load_sem, xs_sem, xr_sem, zs_sem, zr_sem, fs_sem, fr_sem,
):
    me_t = lax.axis_index("theta")
    me_p = lax.axis_index("phi")
    me_b = lax.axis_index("box")

    def load(a):
        return pltpu.make_async_copy(pattern.at[a], pat.at[a], load_sem.at[a])

    for a in range(2):
        load(a).start()

    barrier = pltpu.get_barrier_semaphore()

    def greet_plane(r, carry):
        peer = ((me_t + r // NPHI) % NTHETA, (me_p + r % NPHI) % NPHI, me_b)
        pl.semaphore_signal(barrier, inc=1, device_id=peer, device_id_type=MESH)
        return carry

    def greet_boxes(r, carry):
        peer = ((me_t + r % NTHETA) % NTHETA, me_p, (me_b + r // NTHETA) % NBOX)
        pl.semaphore_signal(barrier, inc=1, device_id=peer, device_id_type=MESH)
        return carry

    lax.fori_loop(1, PLANE, greet_plane, 0)
    lax.fori_loop(NTHETA, NTHETA * NBOX, greet_boxes, 0)

    def box_of(slot):
        group = (me_b + slot + 1) % NBOX
        box = 0
        for b in range(8):
            box = jnp.where(owner[me_b * 8 + b] // 8 == group, b, box)
        return box

    boxes = [box_of(slot) for slot in range(8)]

    def cast(c):
        for half in range(2):
            for a in range(2):
                xsend[c, a * 2 + half] = pat[a, boxes[2 * c + half]].astype(BF)

    def send_x(c):
        for r in range(1, NPHI):
            dest = (me_p + r) % NPHI
            pltpu.make_async_remote_copy(
                src_ref=xsend.at[c, dest], dst_ref=xrecv.at[c, me_p],
                send_sem=xs_sem, recv_sem=xr_sem.at[c],
                device_id=(me_t, dest, me_b), device_id_type=MESH,
            ).start()
        pltpu.make_async_copy(xsend.at[c, me_p], xrecv.at[c, me_p], xr_sem.at[c]).start()

    def transform(c):
        pltpu.make_async_copy(xrecv.at[c], xrecv.at[c], xr_sem.at[c]).wait()

        def rows(m, carry):
            base = pl.multiple_of(m * 256, 256)
            acc = jnp.zeros((256, ROWS), F32)
            for s in range(NPHI):
                acc = acc + dot_nt(trig_v[s, pl.ds(base, 256), :], xrecv[c, s])
            zsend[c, pl.ds(m * 8, 8)] = acc.astype(BF).reshape(8, 2, ORDERS, ROWS)
            return carry

        lax.fori_loop(0, 4, rows, 0)

    def send_z(c):
        def one(r, carry):
            dt, dp = (me_t + r // NPHI) % NTHETA, (me_p + r % NPHI) % NPHI
            pltpu.make_async_remote_copy(
                src_ref=zsend.at[c, dp * NTHETA + dt], dst_ref=zrecv.at[c, me_t, me_p],
                send_sem=zs_sem, recv_sem=zr_sem.at[c],
                device_id=(dt, dp, me_b), device_id_type=MESH,
            ).start()
            return carry

        lax.fori_loop(1, PLANE, one, 0)
        pltpu.make_async_copy(
            zsend.at[c, me_p * NTHETA + me_t], zrecv.at[c, me_t, me_p], zr_sem.at[c]
        ).start()

    sq = (128, 128)
    gather_rows = (iota(sq, 1) == (iota(sq, 0) & 7) * 16 + (iota(sq, 0) >> 3)).astype(BF)
    spread_rows = (iota(sq, 0) == (iota(sq, 1) & 7) * 16 + (iota(sq, 1) >> 3)).astype(BF)
    reverse = (iota(sq, 0) + iota(sq, 1) == 127).astype(BF)
    identity = (iota(sq, 0) == iota(sq, 1)).astype(BF)

    def project(c):
        pltpu.make_async_copy(zrecv.at[c], zrecv.at[c], zr_sem.at[c]).wait()
        for i in range(4):
            north = zrecv[c, i].reshape(128, ROWS)
            south = zrecv[c, 7 - i].reshape(128, ROWS)
            south = dot(south, reverse).astype(BF)
            n_rows = dot(gather_rows, north).reshape(ORDERS, 8, ROWS)
            s_rows = dot(gather_rows, south).reshape(ORDERS, 8, ROWS)
            lhs[:, :, i * ROWS:(i + 1) * ROWS] = jnp.concatenate([n_rows, s_rows], axis=1).astype(BF)

        wide = (8, 512)
        lane, row = iota(wide, 1), iota(wide, 0)
        limit = jnp.where((row & 2) == 0, degree[boxes[2 * c]], degree[boxes[2 * c + 1]])
        keep = lane < limit
        straight = (iota((8, 128), 1) < 64) == (iota((8, 128), 0) < 4)

        def two_orders(h, carry):
            for odd in range(2):
                k = h * 2 + odd
                both = dot(lhs[k], table_v[k])
                north, south = both[:8], both[8:]
                value = jnp.where((lane & 1) == odd, north + south, north - south)
                value = jnp.where(keep, value, 0.0)
                for z in range(4):
                    v = value[:, z * 128:(z + 1) * 128]
                    w = pltpu.roll(pltpu.roll(v, 64, 1), 4, 0)
                    prod[z, pl.ds(pl.multiple_of(k * 8, 8), 8), :] = jnp.where(straight, v, w)
            return carry

        lax.fori_loop(0, ORDERS // 2, two_orders, 0)
        for z in range(4):
            block = dot(spread_rows, prod[z].astype(BF)).astype(BF)
            fsend[c, 2 * z:2 * z + 2] = block.reshape(2, 2, 2, ORDERS, 128)

    def send_f(c):
        def one(half, r):
            group = (me_b + 2 * c + half + 1) % NBOX
            dt = (me_t + r) % NTHETA
            return pltpu.make_async_remote_copy(
                src_ref=fsend.at[c, dt, half], dst_ref=frecv.at[me_b, me_t],
                send_sem=fs_sem, recv_sem=fr_sem,
                device_id=(dt, me_p, group), device_id_type=MESH,
            )

        for half in range(2):
            if (2 * c + half + 1) % NBOX:
                def go(r, carry):
                    one(half, r).start()
                    return carry
                lax.fori_loop(0, NTHETA, go, 0)
            else:
                def go_near(r, carry):
                    one(half, r).start()
                    return carry
                lax.fori_loop(1, NTHETA, go_near, 0)
                pltpu.make_async_copy(
                    fsend.at[c, me_t, half], frecv.at[me_b, me_t], fr_sem
                ).start()

    for a in range(2):
        load(a).wait()
    trig_load = pltpu.make_async_copy(trig, trig_v, load_sem.at[2])
    table_load = pltpu.make_async_copy(table.at[0], table_v, load_sem.at[3])
    trig_load.start()
    cast(0)
    pl.semaphore_wait(barrier, (PLANE - 1) + NTHETA * (NBOX - 1))
    send_x(0)
    cast(1)
    send_x(1)
    table_load.start()
    for c in range(2, CHUNKS):
        cast(c)
    trig_load.wait()
    for c in range(CHUNKS):
        transform(c)
        send_z(c)
        if c + 2 < CHUNKS:
            send_x(c + 2)
        if c == 1:
            table_load.wait()
        if c:
            project(c - 1)
            send_f(c - 1)
    project(CHUNKS - 1)
    send_f(CHUNKS - 1)

    def source_of(q):
        group = 0
        for b in range(64):
            group = jnp.where(owner[b] == me_b * 8 + q, b // 8, group)
        return group

    sources = [source_of(q) for q in range(8)]
    pltpu.make_async_copy(frecv, frecv, fr_sem).wait()
    for q in range(8):
        for s in range(2):
            block = frecv[sources[q], :, s].reshape(128, 128)
            turned = dot_nt(identity, block).astype(BF)
            out[2 * s, q] = turned[:64]
            out[2 * s + 1, q] = turned[64:]

    for c in range(CHUNKS):
        pltpu.make_async_copy(xsend.at[c, pl.ds(0, 3)], xsend.at[c, pl.ds(0, 3)], xs_sem).wait()
        pltpu.make_async_copy(zsend.at[c, pl.ds(0, 31)], zsend.at[c, pl.ds(0, 31)], zs_sem).wait()
    part = fsend.at[pl.ds(0, 3)]
    pltpu.make_async_copy(part, part, fs_sem).wait()
    part = fsend.at[3, pl.ds(0, 7)]
    pltpu.make_async_copy(part, part, fs_sem).wait()
    part = fsend.at[3, 7, 0]
    pltpu.make_async_copy(part, part, fs_sem).wait()


def local(pattern, legendre, degree, owner):
    any_space = pl.BlockSpec(memory_space=pl.ANY)
    smem = pl.BlockSpec(memory_space=pltpu.SMEM)
    vmem = pl.BlockSpec(memory_space=pltpu.VMEM)
    dma = pltpu.SemaphoreType.DMA
    return pl.pallas_call(
        kernel,
        out_shape=jax.ShapeDtypeStruct((4, 8, 64, 128), BF),
        in_specs=[any_space, any_space, any_space, smem, smem],
        out_specs=vmem,
        scratch_shapes=[
            pltpu.VMEM((2, 8, ROWS, COLS), F32),
            pltpu.VMEM((CHUNKS, NPHI, ROWS, COLS), BF),
            pltpu.VMEM((CHUNKS, NPHI, ROWS, COLS), BF),
            pltpu.VMEM((NPHI, PLANE * 2 * ORDERS, COLS), BF),
            pltpu.VMEM((ORDERS, 512, 512), BF),
            pltpu.VMEM((CHUNKS, PLANE, 2, ORDERS, ROWS), BF),
            pltpu.VMEM((CHUNKS, NTHETA, NPHI, 2, ORDERS, ROWS), BF),
            pltpu.VMEM((ORDERS, 16, 512), BF),
            pltpu.VMEM((4, 128, 128), F32),
            pltpu.VMEM((CHUNKS, NTHETA, 2, 2, ORDERS, 128), BF),
            pltpu.VMEM((NBOX, NTHETA, 2, ORDERS, 128), BF),
            dma((4,)), dma, dma((CHUNKS,)), dma, dma((CHUNKS,)), dma, dma,
        ],
        compiler_params=pltpu.CompilerParams(
            collective_id=0, has_side_effects=True, vmem_limit_bytes=48 * 1024 * 1024
        ),
        cost_estimate=pl.CostEstimate(
            flops=2_700_000_000, bytes_accessed=17_000_000, transcendentals=0
        ),
    )(pattern, jnp.asarray(trig_table()), legendre, degree, owner)


def solution(mesh):
    in_specs = (P(None, "box", "theta", "phi"), P("phi", "theta", None, None), P("box"), P())
    out_specs = P(None, "box", "theta", "phi")
    return jax.shard_map(local, mesh=mesh, in_specs=in_specs, out_specs=out_specs, check_vma=False)
```

time: 314 us -> 72.6 us (0.23)
  waiting for transfers between devices: 152 us -> 0 us
  local copies, waits for them, and re-layouts: 83.7 us -> 4.29 us
  Pallas kernels: 0 us -> 68.1 us
  starting transfers between devices: 21.8 us -> 0 us
  blocking collectives: 20.7 us -> 0 us
  matrix products: 20.4 us -> 0 us
  other arithmetic: 12.8 us -> 0 us
    all_to_all x2 -> x0, waiting for transfers between devices: 152 us -> none  [the longest x1 146 us: local(): lax.all_to_all(partial_terms, ('theta', 'phi'), split_axis=0, concat_axis...]
    pallas_call x0 -> x1, Pallas kernels: none -> 68.1 us  [local(): pl.pallas_call(kernel, out_shape=jax.ShapeDtypeStruct((4, 8, 64, 128), BF...]
    unnamed x12 -> x7, local copies, waits for them, and re-layouts: 39.9 us -> 4.29 us
    all_to_all x2 -> x0, starting transfers between devices: 21.8 us -> none  [the longest x1 12.8 us: local(): lax.all_to_all(partial_terms, ('theta', 'phi'), split_axis=0, concat_axis...]
    all_to_all x1 -> x0, blocking collectives: 20.7 us -> none  [local(): lax.all_to_all(outgoing, 'theta', split_axis=2, concat_axis=3, tiled=True)]
    dot_general x3 -> x0, matrix products: 20.4 us -> none  [the longest x1 16.4 us: local(): jnp.einsum('skp,abtp->ksabt', trig_table, pattern, precision=lax.Precisio...]
    reshape x5 -> x0, local copies, waits for them, and re-layouts: 14.5 us -> none  [the longest x1 8.07 us: local(): partial_terms = terms.reshape(all_orders, 4, box_count, pattern.shape[2])]
    slice x2 -> x0, local copies, waits for them, and re-layouts: 7.04 us -> none  [the longest x1 5.94 us: local(): tables[..., 0]]
  transfers between devices with their start and end apart: 2 -> 0, of which waited for: 2 -> 0; matrix products, arithmetic and copies ran while one was open for 12% -> 0% of each run, Pallas kernels for 0% -> 0%
where the time goes in v1:
time: 72.6 us; the launch traced here: 72.4 us
  Pallas kernels  68.1 us (94%)
  local copies, waits for them, and re-layouts  4.29 us (6%)
    pallas_call x1, Pallas kernels, local(): pl.pallas_call(kernel, out_shape=jax.ShapeDtypeStruct((4, 8, 64, 128), BF...  68.1 us
    unnamed x7, local copies, waits for them, and re-layouts  4.29 us

profile of v1, /device:TPU:1, one launch (start us, length us, event | category | flops | bytes accessed | tf_op | source)
XLA Modules:
  0.0 72.4 jit_solution(7029293870129110603)
XLA Ops:
  0.0 0.0 copy-start
  0.0 2.2 %copy-done = f32[2,8,128,512]{3,2,1,0:T(8,128)S(1)} copy-done((f32[2,8,128,512]{3,2,1,0:T(8,128)S(1)}, f32[2,8,128,512]{3,2,1,0:T(8,128)}, u32[]{:S(2)}) %copy-start) | copy-done | bytes 4194328
  2.2 0.0 copy-start.1
  2.2 0.7 copy-done.1
  2.8 0.0 copy-start.2
  2.8 0.7 copy-done.2
  3.5 68.1 %shard_map.55 = bf16[4,8,64,128]{3,2,1,0:T(8,128)(2,1)S(1)} custom-call(f32[2,8,128,512]{3,2,1,0:T(8,128)S(1)} %copy-done, bf16[4,1024,512]{2,1,0:T(8,128)(2,1)} %constant.2.clone.trig, bf16[1,16,512,512]{3,2,1,0:T(8,128)(2,1)} %table.1, s32[8]{0:T(128)S(1)} %copy-done.1, s32[64]{0:T(128)S(1)} %copy-done.2), custom_call_target="tpu_custom_call" | custom-call | flops 2700000000 | bytes 17000000 | tf_op jit(solution)/shard_map/pallas_call | solution.py:249
  71.6 0.8 %copy.7 = bf16[4,8,64,128]{3,2,1,0:T(8,128)(2,1)} copy(bf16[4,8,64,128]{3,2,1,0:T(8,128)(2,1)S(1)} %shard_map.55) | data formatting | bytes 1048576
Async XLA Ops:
  0.0 2.2 %copy-start = (f32[2,8,128,512]{3,2,1,0:T(8,128)S(1)}, f32[2,8,128,512]{3,2,1,0:T(8,128)}, u32[]{:S(2)}) copy-start(f32[2,8,128,512]{3,2,1,0:T(8,128)} %pattern.1) | copy-start | bytes 12582916
  2.2 0.7 copy-start.1
  2.8 0.7 copy-start.2

commit v2 on v1

--- a/solution.py
+++ b/solution.py
@@ -43,8 +43,8 @@
 
 def kernel(
     pattern, trig, table, degree, owner, out,
-    pat, xsend, xrecv, trig_v, table_v, zsend, zrecv, lhs, prod, fsend, frecv,
-    load_sem, xs_sem, xr_sem, zs_sem, zr_sem, fs_sem, fr_sem,
+    pat, xsend, xrecv, trig_v, table_v, zsend, zrecv, lhs, prod, fsend, frecv, turned,
+    load_sem, plane_sem, xs_sem, xr_sem, zs_sem, zr_sem, fs_sem, fr_sem,
 ):
     me_t = lax.axis_index("theta")
     me_p = lax.axis_index("phi")
@@ -58,18 +58,19 @@
 
     barrier = pltpu.get_barrier_semaphore()
 
-    def greet_plane(r, carry):
-        peer = ((me_t + r // NPHI) % NTHETA, (me_p + r % NPHI) % NPHI, me_b)
-        pl.semaphore_signal(barrier, inc=1, device_id=peer, device_id_type=MESH)
-        return carry
-
-    def greet_boxes(r, carry):
-        peer = ((me_t + r % NTHETA) % NTHETA, me_p, (me_b + r // NTHETA) % NBOX)
-        pl.semaphore_signal(barrier, inc=1, device_id=peer, device_id_type=MESH)
-        return carry
-
-    lax.fori_loop(1, PLANE, greet_plane, 0)
-    lax.fori_loop(NTHETA, NTHETA * NBOX, greet_boxes, 0)
+    def greet(semaphore, axis, size):
+        mine = {"theta": me_t, "phi": me_p, "box": me_b}
+        for r in range(1, size):
+            peer = dict(mine)
+            peer[axis] = (mine[axis] + r) % size
+            pl.semaphore_signal(
+                semaphore, inc=1, device_id=(peer["theta"], peer["phi"], peer["box"]),
+                device_id_type=MESH,
+            )
+
+    greet(barrier, "phi", NPHI)
+    greet(barrier, "theta", NTHETA)
+    greet(barrier, "box", NBOX)
 
     def box_of(slot):
         group = (me_b + slot + 1) % NBOX
@@ -98,27 +99,35 @@
     def transform(c):
         pltpu.make_async_copy(xrecv.at[c], xrecv.at[c], xr_sem.at[c]).wait()
 
-        def rows(m, carry):
-            base = pl.multiple_of(m * 256, 256)
-            acc = jnp.zeros((256, ROWS), F32)
-            for s in range(NPHI):
+        def group(g, carry):
+            dp = (me_p + 1 + g) % NPHI
+            base = pl.multiple_of(dp * 256, 256)
+            acc = dot_nt(trig_v[0, pl.ds(base, 256), :], xrecv[c, 0])
+            for s in range(1, NPHI):
                 acc = acc + dot_nt(trig_v[s, pl.ds(base, 256), :], xrecv[c, s])
-            zsend[c, pl.ds(m * 8, 8)] = acc.astype(BF).reshape(8, 2, ORDERS, ROWS)
+            zsend[c, pl.ds(dp * NTHETA, NTHETA)] = acc.astype(BF).reshape(NTHETA, 2, ORDERS, ROWS)
+            if c == 0:
+                @pl.when(g == 0)
+                def _():
+                    pl.semaphore_wait(plane_sem, NTHETA - 1)
+
+            def one(r, carry):
+                dt = (me_t + r) % NTHETA
+                pltpu.make_async_remote_copy(
+                    src_ref=zsend.at[c, dp * NTHETA + dt], dst_ref=zrecv.at[c, me_t, me_p],
+                    send_sem=zs_sem, recv_sem=zr_sem.at[c],
+                    device_id=(dt, dp, me_b), device_id_type=MESH,
+                ).start()
+                return carry
+
+            lax.fori_loop(1, NTHETA, one, 0)
+
+            @pl.when(g < NPHI - 1)
+            def _():
+                one(0, 0)
             return carry
 
-        lax.fori_loop(0, 4, rows, 0)
-
-    def send_z(c):
-        def one(r, carry):
-            dt, dp = (me_t + r // NPHI) % NTHETA, (me_p + r % NPHI) % NPHI
-            pltpu.make_async_remote_copy(
-                src_ref=zsend.at[c, dp * NTHETA + dt], dst_ref=zrecv.at[c, me_t, me_p],
-                send_sem=zs_sem, recv_sem=zr_sem.at[c],
-                device_id=(dt, dp, me_b), device_id_type=MESH,
-            ).start()
-            return carry
-
-        lax.fori_loop(1, PLANE, one, 0)
+        lax.fori_loop(0, NPHI, group, 0)
         pltpu.make_async_copy(
             zsend.at[c, me_p * NTHETA + me_t], zrecv.at[c, me_t, me_p], zr_sem.at[c]
         ).start()
@@ -139,54 +148,63 @@
             s_rows = dot(gather_rows, south).reshape(ORDERS, 8, ROWS)
             lhs[:, :, i * ROWS:(i + 1) * ROWS] = jnp.concatenate([n_rows, s_rows], axis=1).astype(BF)
 
-        wide = (8, 512)
+        wide = (8, 256)
         lane, row = iota(wide, 1), iota(wide, 0)
         limit = jnp.where((row & 2) == 0, degree[boxes[2 * c]], degree[boxes[2 * c + 1]])
-        keep = lane < limit
         straight = (iota((8, 128), 1) < 64) == (iota((8, 128), 0) < 4)
 
-        def two_orders(h, carry):
-            for odd in range(2):
-                k = h * 2 + odd
-                both = dot(lhs[k], table_v[k])
-                north, south = both[:8], both[8:]
-                value = jnp.where((lane & 1) == odd, north + south, north - south)
-                value = jnp.where(keep, value, 0.0)
-                for z in range(4):
-                    v = value[:, z * 128:(z + 1) * 128]
-                    w = pltpu.roll(pltpu.roll(v, 64, 1), 4, 0)
-                    prod[z, pl.ds(pl.multiple_of(k * 8, 8), 8), :] = jnp.where(straight, v, w)
+        for nh in range(2):
+            def two_orders(h, carry):
+                for odd in range(2):
+                    k = h * 2 + odd
+                    both = dot(lhs[k], table_v[k, :, nh * 256:(nh + 1) * 256])
+                    north, south = both[:8], both[8:]
+                    value = jnp.where((lane & 1) == odd, north + south, north - south)
+                    value = jnp.where(lane + nh * 256 < limit, value, 0.0)
+                    for z in range(2):
+                        v = value[:, z * 128:(z + 1) * 128]
+                        w = pltpu.roll(pltpu.roll(v, 64, 1), 4, 0)
+                        at = pl.ds(pl.multiple_of(k * 8, 8), 8)
+                        prod[nh * 2 + z, at, :] = jnp.where(straight, v, w)
+                return carry
+
+            lax.fori_loop(0, ORDERS // 2, two_orders, 0, unroll=True)
+            for z in range(2 * nh, 2 * nh + 2):
+                block = dot(spread_rows, prod[z].astype(BF)).astype(BF)
+                fsend[c, 2 * z:2 * z + 2] = block.reshape(2, 2, 2, ORDERS, 128)
+            for half in range(2):
+                send_f(c, nh, half)
+
+    def send_f(c, nh, half):
+        group = (me_b + 2 * c + half + 1) % NBOX
+        near = (2 * c + half + 1) % NBOX == 0
+
+        def one(r, carry):
+            dt = nh * 4 + (me_t + r) % 4
+            def go():
+                pltpu.make_async_remote_copy(
+                    src_ref=fsend.at[c, dt, half], dst_ref=frecv.at[me_b, me_t],
+                    send_sem=fs_sem, recv_sem=fr_sem.at[c],
+                    device_id=(dt, me_p, group), device_id_type=MESH,
+                ).start()
+            if near:
+                pl.when(dt != me_t)(go)
+            else:
+                go()
             return carry
 
-        lax.fori_loop(0, ORDERS // 2, two_orders, 0)
-        for z in range(4):
-            block = dot(spread_rows, prod[z].astype(BF)).astype(BF)
-            fsend[c, 2 * z:2 * z + 2] = block.reshape(2, 2, 2, ORDERS, 128)
-
-    def send_f(c):
-        def one(half, r):
-            group = (me_b + 2 * c + half + 1) % NBOX
-            dt = (me_t + r) % NTHETA
-            return pltpu.make_async_remote_copy(
-                src_ref=fsend.at[c, dt, half], dst_ref=frecv.at[me_b, me_t],
-                send_sem=fs_sem, recv_sem=fr_sem,
-                device_id=(dt, me_p, group), device_id_type=MESH,
-            )
-
+        lax.fori_loop(0, 4, one, 0)
+        if near and nh:
+            pltpu.make_async_copy(fsend.at[c, me_t, half], frecv.at[me_b, me_t], fr_sem.at[c]).start()
+
+    def finish(c):
+        pltpu.make_async_copy(fsend.at[c], fsend.at[c], fr_sem.at[c]).wait()
         for half in range(2):
-            if (2 * c + half + 1) % NBOX:
-                def go(r, carry):
-                    one(half, r).start()
-                    return carry
-                lax.fori_loop(0, NTHETA, go, 0)
-            else:
-                def go_near(r, carry):
-                    one(half, r).start()
-                    return carry
-                lax.fori_loop(1, NTHETA, go_near, 0)
-                pltpu.make_async_copy(
-                    fsend.at[c, me_t, half], frecv.at[me_b, me_t], fr_sem
-                ).start()
+            slot = (2 * c + half + 1) % NBOX
+            source = (me_b + NBOX - slot) % NBOX
+            for s in range(2):
+                block = frecv[source, :, s].reshape(128, 128)
+                turned[slot, s] = dot_nt(identity, block).astype(BF)
 
     for a in range(2):
         load(a).wait()
@@ -194,8 +212,9 @@
     table_load = pltpu.make_async_copy(table.at[0], table_v, load_sem.at[3])
     trig_load.start()
     cast(0)
-    pl.semaphore_wait(barrier, (PLANE - 1) + NTHETA * (NBOX - 1))
+    pl.semaphore_wait(barrier, NPHI + NTHETA + NBOX - 3)
     send_x(0)
+    greet(plane_sem, "theta", NTHETA)
     cast(1)
     send_x(1)
     table_load.start()
@@ -204,16 +223,16 @@
     trig_load.wait()
     for c in range(CHUNKS):
         transform(c)
-        send_z(c)
         if c + 2 < CHUNKS:
             send_x(c + 2)
         if c == 1:
             table_load.wait()
         if c:
             project(c - 1)
-            send_f(c - 1)
+        if c > 1:
+            finish(c - 2)
     project(CHUNKS - 1)
-    send_f(CHUNKS - 1)
+    finish(CHUNKS - 2)
 
     def source_of(q):
         group = 0
@@ -221,14 +240,12 @@
             group = jnp.where(owner[b] == me_b * 8 + q, b // 8, group)
         return group
 
-    sources = [source_of(q) for q in range(8)]
-    pltpu.make_async_copy(frecv, frecv, fr_sem).wait()
+    slots = [(me_b + NBOX - source_of(q)) % NBOX for q in range(8)]
+    finish(CHUNKS - 1)
     for q in range(8):
         for s in range(2):
-            block = frecv[sources[q], :, s].reshape(128, 128)
-            turned = dot_nt(identity, block).astype(BF)
-            out[2 * s, q] = turned[:64]
-            out[2 * s + 1, q] = turned[64:]
+            out[2 * s, q] = turned[slots[q], s, :64]
+            out[2 * s + 1, q] = turned[slots[q], s, 64:]
 
     for c in range(CHUNKS):
         pltpu.make_async_copy(xsend.at[c, pl.ds(0, 3)], xsend.at[c, pl.ds(0, 3)], xs_sem).wait()
@@ -263,10 +280,12 @@
             pltpu.VMEM((4, 128, 128), F32),
             pltpu.VMEM((CHUNKS, NTHETA, 2, 2, ORDERS, 128), BF),
             pltpu.VMEM((NBOX, NTHETA, 2, ORDERS, 128), BF),
-            dma((4,)), dma, dma((CHUNKS,)), dma, dma((CHUNKS,)), dma, dma,
+            pltpu.VMEM((NBOX, 2, 128, 128), BF),
+            dma((4,)), pltpu.SemaphoreType.REGULAR,
+            dma, dma((CHUNKS,)), dma, dma((CHUNKS,)), dma, dma((CHUNKS,)),
         ],
         compiler_params=pltpu.CompilerParams(
-            collective_id=0, has_side_effects=True, vmem_limit_bytes=48 * 1024 * 1024
+            collective_id=0, has_side_effects=True, vmem_limit_bytes=60 * 1024 * 1024
         ),
         cost_estimate=pl.CostEstimate(
             flops=2_700_000_000, bytes_accessed=17_000_000, transcendentals=0

time: 72.6 us -> 64.7 us (0.89)
  Pallas kernels: 68.1 us -> 62.7 us
  local copies, waits for them, and re-layouts: 4.29 us -> 1.87 us
    pallas_call x1, Pallas kernels: 68.1 us -> 62.7 us  [local(): pl.pallas_call(kernel, out_shape=jax.ShapeDtypeStruct((4, 8, 64, 128), BF...]
    unnamed x7 -> x1, local copies, waits for them, and re-layouts: 4.29 us -> 1.87 us
where the time goes in v2:
time: 64.7 us; the launch traced here: 64.6 us
  Pallas kernels  62.7 us (97%)
  local copies, waits for them, and re-layouts  1.87 us (3%)
    pallas_call x1, Pallas kernels, local(): pl.pallas_call(kernel, out_shape=jax.ShapeDtypeStruct((4, 8, 64, 128), BF...  62.7 us
    unnamed x1, local copies, waits for them, and re-layouts  1.87 us

profile of v2, /device:TPU:1, one launch (start us, length us, event | category | flops | bytes accessed | tf_op | source)
XLA Modules:
  0.0 64.6 jit_solution(13319544075218106127)
XLA Ops:
  0.0 62.7 %shard_map.55 = bf16[4,8,64,128]{3,2,1,0:T(8,128)(2,1)} custom-call(f32[2,8,128,512]{3,2,1,0:T(8,128)} %pattern.1, bf16[4,1024,512]{2,1,0:T(8,128)(2,1)} %constant.2.clone.trig, bf16[1,16,512,512]{3,2,1,0:T(8,128)(2,1)} %table.1, s32[8]{0:T(128)} %degree.1, s32[64]{0:T(128)} %owner.1), custom_call_target="tpu_custom_call" | custom-call | flops 2700000000 | bytes 17000000 | tf_op jit(solution)/shard_map/pallas_call | solution.py:266
  62.7 1.9 %copy.7 = bf16[4,8,64,128]{3,2,1,0:T(8,128)(2,1)} copy(bf16[4,8,64,128]{3,2,1,0:T(8,128)(2,1)} %shard_map.55) | data formatting | bytes 1048576

commit v3 on v2

--- a/solution.py
+++ b/solution.py
@@ -87,7 +87,7 @@
                 xsend[c, a * 2 + half] = pat[a, boxes[2 * c + half]].astype(BF)
 
     def send_x(c):
-        for r in range(1, NPHI):
+        for r in (2, 1, 3):
             dest = (me_p + r) % NPHI
             pltpu.make_async_remote_copy(
                 src_ref=xsend.at[c, dest], dst_ref=xrecv.at[c, me_p],
@@ -140,6 +140,8 @@
 
     def project(c):
         pltpu.make_async_copy(zrecv.at[c], zrecv.at[c], zr_sem.at[c]).wait()
+        if c + 3 < CHUNKS:
+            send_x(c + 3)
         for i in range(4):
             north = zrecv[c, i].reshape(128, ROWS)
             south = zrecv[c, 7 - i].reshape(128, ROWS)
@@ -223,8 +225,8 @@
     trig_load.wait()
     for c in range(CHUNKS):
         transform(c)
-        if c + 2 < CHUNKS:
-            send_x(c + 2)
+        if c == 0:
+            send_x(2)
         if c == 1:
             table_load.wait()
         if c:

time: 64.7 us -> 63.8 us (0.986)
  Pallas kernels: 62.7 us -> 61.8 us
    pallas_call x1, Pallas kernels: 62.7 us -> 61.8 us  [local(): pl.pallas_call(kernel, out_shape=jax.ShapeDtypeStruct((4, 8, 64, 128), BF...]
where the time goes in v3:
time: 63.8 us; the launch traced here: 63.6 us
  Pallas kernels  61.8 us (97%)
  local copies, waits for them, and re-layouts  1.87 us (3%)
    pallas_call x1, Pallas kernels, local(): pl.pallas_call(kernel, out_shape=jax.ShapeDtypeStruct((4, 8, 64, 128), BF...  61.8 us
    unnamed x1, local copies, waits for them, and re-layouts  1.87 us

profile of v3, /device:TPU:1, one launch (start us, length us, event | category | flops | bytes accessed | tf_op | source)
XLA Modules:
  0.0 63.6 jit_solution(12032109710110656233)
XLA Ops:
  0.0 61.8 %shard_map.55 = bf16[4,8,64,128]{3,2,1,0:T(8,128)(2,1)} custom-call(f32[2,8,128,512]{3,2,1,0:T(8,128)} %pattern.1, bf16[4,1024,512]{2,1,0:T(8,128)(2,1)} %constant.2.clone.trig, bf16[1,16,512,512]{3,2,1,0:T(8,128)(2,1)} %table.1, s32[8]{0:T(128)} %degree.1, s32[64]{0:T(128)} %owner.1), custom_call_target="tpu_custom_call" | custom-call | flops 2700000000 | bytes 17000000 | tf_op jit(solution)/shard_map/pallas_call | solution.py:268
  61.8 1.9 %copy.7 = bf16[4,8,64,128]{3,2,1,0:T(8,128)(2,1)} copy(bf16[4,8,64,128]{3,2,1,0:T(8,128)(2,1)} %shard_map.55) | data formatting | bytes 1048576

commit v4 on v3

--- a/solution.py
+++ b/solution.py
@@ -112,7 +112,7 @@
                     pl.semaphore_wait(plane_sem, NTHETA - 1)
 
             def one(r, carry):
-                dt = (me_t + r) % NTHETA
+                dt = (me_t + 3 + r) % NTHETA
                 pltpu.make_async_remote_copy(
                     src_ref=zsend.at[c, dp * NTHETA + dt], dst_ref=zrecv.at[c, me_t, me_p],
                     send_sem=zs_sem, recv_sem=zr_sem.at[c],
@@ -120,11 +120,12 @@
                 ).start()
                 return carry
 
-            lax.fori_loop(1, NTHETA, one, 0)
+            lax.fori_loop(0, 5, one, 0)
+            lax.fori_loop(6, NTHETA, one, 0)
 
             @pl.when(g < NPHI - 1)
             def _():
-                one(0, 0)
+                one(5, 0)
             return carry
 
         lax.fori_loop(0, NPHI, group, 0)
@@ -182,7 +183,7 @@
         near = (2 * c + half + 1) % NBOX == 0
 
         def one(r, carry):
-            dt = nh * 4 + (me_t + r) % 4
+            dt = nh * 4 + (me_t + 2 + r) % 4
             def go():
                 pltpu.make_async_remote_copy(
                     src_ref=fsend.at[c, dt, half], dst_ref=frecv.at[me_b, me_t],

time: 63.8 us -> 63.5 us (level)
  no operation moved by 1% of the time
where the time goes in v4:
time: 63.5 us; the launch traced here: 63.3 us
  Pallas kernels  61.5 us (97%)
  local copies, waits for them, and re-layouts  1.87 us (3%)
    pallas_call x1, Pallas kernels, local(): pl.pallas_call(kernel, out_shape=jax.ShapeDtypeStruct((4, 8, 64, 128), BF...  61.5 us
    unnamed x1, local copies, waits for them, and re-layouts  1.87 us

profile of v4, /device:TPU:1, one launch (start us, length us, event | category | flops | bytes accessed | tf_op | source)
XLA Modules:
  0.0 63.3 jit_solution(2416078395577504043)
XLA Ops:
  0.0 61.5 %shard_map.55 = bf16[4,8,64,128]{3,2,1,0:T(8,128)(2,1)} custom-call(f32[2,8,128,512]{3,2,1,0:T(8,128)} %pattern.1, bf16[4,1024,512]{2,1,0:T(8,128)(2,1)} %constant.2.clone.trig, bf16[1,16,512,512]{3,2,1,0:T(8,128)(2,1)} %table.1, s32[8]{0:T(128)} %degree.1, s32[64]{0:T(128)} %owner.1), custom_call_target="tpu_custom_call" | custom-call | flops 2700000000 | bytes 17000000 | tf_op jit(solution)/shard_map/pallas_call | solution.py:269
  61.5 1.9 %copy.7 = bf16[4,8,64,128]{3,2,1,0:T(8,128)(2,1)} copy(bf16[4,8,64,128]{3,2,1,0:T(8,128)(2,1)} %shard_map.55) | data formatting | bytes 1048576

commit v5 on v4

--- a/solution.py
+++ b/solution.py
@@ -100,7 +100,7 @@
         pltpu.make_async_copy(xrecv.at[c], xrecv.at[c], xr_sem.at[c]).wait()
 
         def group(g, carry):
-            dp = (me_p + 1 + g) % NPHI
+            dp = (me_p + g) % NPHI
             base = pl.multiple_of(dp * 256, 256)
             acc = dot_nt(trig_v[0, pl.ds(base, 256), :], xrecv[c, 0])
             for s in range(1, NPHI):
@@ -123,7 +123,7 @@
             lax.fori_loop(0, 5, one, 0)
             lax.fori_loop(6, NTHETA, one, 0)
 
-            @pl.when(g < NPHI - 1)
+            @pl.when(g > 0)
             def _():
                 one(5, 0)
             return carry

time: 63.5 us -> 63.8 us (level)
  no operation moved by 1% of the time
where the time goes in v5:
time: 63.8 us; the launch traced here: 63.7 us
  Pallas kernels  61.8 us (97%)
  local copies, waits for them, and re-layouts  1.87 us (3%)
    pallas_call x1, Pallas kernels, local(): pl.pallas_call(kernel, out_shape=jax.ShapeDtypeStruct((4, 8, 64, 128), BF...  61.8 us
    unnamed x1, local copies, waits for them, and re-layouts  1.87 us

profile of v5, /device:TPU:1, one launch (start us, length us, event | category | flops | bytes accessed | tf_op | source)
XLA Modules:
  0.0 63.7 jit_solution(16128758654325369320)
XLA Ops:
  0.0 61.8 %shard_map.55 = bf16[4,8,64,128]{3,2,1,0:T(8,128)(2,1)} custom-call(f32[2,8,128,512]{3,2,1,0:T(8,128)} %pattern.1, bf16[4,1024,512]{2,1,0:T(8,128)(2,1)} %constant.2.clone.trig, bf16[1,16,512,512]{3,2,1,0:T(8,128)(2,1)} %table.1, s32[8]{0:T(128)} %degree.1, s32[64]{0:T(128)} %owner.1), custom_call_target="tpu_custom_call" | custom-call | flops 2700000000 | bytes 17000000 | tf_op jit(solution)/shard_map/pallas_call | solution.py:269
  61.8 1.9 %copy.7 = bf16[4,8,64,128]{3,2,1,0:T(8,128)(2,1)} copy(bf16[4,8,64,128]{3,2,1,0:T(8,128)(2,1)} %shard_map.55) | data formatting | bytes 1048576
